TPU v7x, 32 devices: a whole 2x2x4 slice. The times are simulated.
32 devices in a mesh: dp: 8 (over z, x), work: 4 (over y, core).
Axes of the slice: x: 2, y: 2, z: 4, core: 2. Of those that a mesh axis runs over, the one named last changes fastest.
Arguments:
- act_one: bfloat16 [1024, 5120], P('dp', 'work')
- grad_one: bfloat16 [1024, 5120], P('dp', 'work')
- act_two: bfloat16 [1024, 5120], P('dp', 'work')
- grad_two: bfloat16 [1024, 5120], P('dp', 'work')
- owner_table: int32 [4, 6], replicated, may hold values from -1 to 79, as said below
Outputs:
- eigen_blocks: float32 [4, 6, 256, 256], replicated
Inputs may be any that keep to these rules, and one draw needn't show every extreme that they name: `owner_table`: an entry names factor block f * 20 + k (block k of input f) or is -1 for an empty slot. Exactly 12 slots are filled, no block appears twice, and at least one owner has all 6 slots filled. Block k's features lie on work member (k mod (20)) // (5120 / (256 * 4)); no member holds more than 6 filled blocks, and one member holds exactly 6.
All inputs are finite; a program needn't handle non-finite values.
Results may differ from a plain program's by a relative error of at most 0.0003.
Values sent between devices are 32-bit elements; how exact they have to be, the bound alone decides.
A program may use at most 64 MiB of HBM per device.

v0:
```python
import math

import jax
import jax.numpy as jnp
from jax import lax
from jax.sharding import PartitionSpec as P

BS = 256
ITERS = 4


DAMPING = 0.1


def block_grams(features):
    tok_rows, feature_width = features.shape
    shaped = features.reshape(tok_rows, feature_width // BS, BS)
    return jnp.einsum("tkb,tkc->kbc", shaped, shaped, preferred_element_type=jnp.float32)


def orthogonal_steps(factor):
    eigen_basis = jnp.broadcast_to(jnp.eye(factor.shape[-1], dtype=jnp.float32), factor.shape)
    for iteration in range(ITERS):
        projected = jnp.matmul(factor, eigen_basis, precision=lax.Precision.HIGHEST)
        inner_gram = jnp.matmul(
            jnp.swapaxes(projected, -1, -2), projected, precision=lax.Precision.HIGHEST
        )
        lower_factor = lax.linalg.cholesky(inner_gram)
        eigen_basis = lax.linalg.triangular_solve(
            lower_factor, projected, left_side=False, lower=True, transpose_a=True
        )
    return eigen_basis


def local_rows(block_id, per_holder, per_factor):
    within_factor = block_id % per_factor
    return (
        block_id // per_factor * per_holder + within_factor % per_holder,
        within_factor // per_holder,
    )


def route(stacked, assignment, member, per_holder, per_factor):
    usable = assignment >= 0
    block_id = jnp.maximum(assignment, 0)
    local_row, holder = local_rows(block_id, per_holder, per_factor)
    picked = stacked[local_row]
    keeping = usable & (holder == member)
    outgoing = jnp.where(keeping[:, :, None, None], picked, 0.0)
    incoming = lax.all_to_all(outgoing, "work", split_axis=0, concat_axis=0, tiled=True)
    return jnp.sum(incoming, axis=0)


def per_device(act_one, grad_one, act_two, grad_two, owner_table):
    workers = lax.axis_size("work")
    tok_rows, feature_width = act_one.shape
    tokens_all = tok_rows * lax.axis_size("dp")
    per_holder = feature_width // BS
    per_factor = per_holder * workers
    member = lax.axis_index("work")
    slot_count = owner_table.shape[1]
    flat_table = owner_table.reshape(-1)
    flat_count = flat_table.shape[0]
    filled = flat_table >= 0
    gathered_index = jnp.arange(flat_count, dtype=jnp.int32)
    live_slots = owner_table[member] >= 0
    stacked = jnp.concatenate(
        [block_grams(source) for source in (act_one, grad_one, act_two, grad_two)], axis=0
    )
    owned_factors = lax.psum(route(stacked, owner_table, member, per_holder, per_factor), "dp")
    identity = jnp.eye(BS, dtype=jnp.float32)
    scaled = owned_factors / tokens_all
    mean_diag = jnp.trace(scaled, axis1=1, axis2=2) / BS
    factor = scaled + DAMPING * mean_diag[:, None, None] * identity
    factor = jnp.where(live_slots[:, None, None], factor, identity)
    eigen_basis = orthogonal_steps(factor) * math.sqrt(BS)
    eigen_basis = jnp.where(live_slots[:, None, None], eigen_basis, 0.0)
    all_bases = lax.all_gather(eigen_basis, "work", axis=0, tiled=True)
    placed = all_bases[gathered_index]
    placed = jnp.where(filled[:, None, None], placed, 0.0)
    return placed.reshape(workers, slot_count, BS, BS)


def solution(mesh):
    in_specs = (P("dp", "work"), P("dp", "work"), P("dp", "work"), P("dp", "work"), P())
    out_specs = P()
    return jax.shard_map(
        per_device, mesh=mesh, in_specs=in_specs, out_specs=out_specs, check_vma=False
    )
```

profile of v0, /device:TPU:0, one launch (start us, length us, event | category | flops | bytes accessed | tf_op | source)
XLA Modules:
  0.0 1726.3 jit_solution(10805158639552051743)
XLA Ops:
  36.3 71.3 %all-to-all-done = f32[4,6,256,256]{3,2,1,0:T(8,128)} async-done(((f32[4,6,256,256]{3,2,1,0:T(8,128)}), f32[4,6,256,256]{3,2,1,0:T(8,128)}, u32[]{:S(2)}, u32[]{:S(2)}) %all-to-all-start) | async-done | bytes 6291488 | tf_op jit(solution)/shard_map/all_to_all | solution.py:50
  113.1 89.3 %all-reduce.3.cloned.1.call-done = f32[6,256,256]{2,1,0:T(8,128)} async-done(((f32[6,256,256]{2,1,0:T(8,128)}), f32[6,256,256]{2,1,0:T(8,128)}) %all-reduce.3.cloned.1.call-update) | async-done | bytes 1572880 | tf_op jit(solution)/shard_map/psum | solution.py:70
  216.9 72.0 %custom-call.25 = f32[6,128,128]{2,1,0:T(8,128)} custom-call(f32[6,128,128]{2,1,0:T(8,128)} %slice.114), custom_call_target="Cholesky" | custom-call | tf_op jit(solution)/shard_map/cholesky/custom-call.2 | solution.py:28
  290.6 60.4 %custom-call.26 = f32[6,1,128,128]{2,3,1,0:T(8,128)} custom-call(f32[6,1,128,128]{3,2,1,0:T(8,128)} %select_bitcast_fusion.3), custom_call_target="InvertDiagBlocksLowerTriangular" | custom-call | tf_op jit(solution)/shard_map/cholesky/custom-call.4 | solution.py:28
  359.8 72.2 %custom-call.27 = f32[6,128,128]{2,1,0:T(8,128)} custom-call(f32[6,128,128]{2,1,0:T(8,128)} %convolution_subtract_fusion.7), custom_call_target="Cholesky" | custom-call | tf_op jit(solution)/shard_map/cholesky/custom-call.3 | solution.py:28
  439.6 7.7 while.8
  447.3 119.3 %custom-call.28 = f32[6,2,128,128]{2,3,1,0:T(8,128)} custom-call(f32[6,2,128,128]{3,2,1,0:T(8,128)} %bitcast.183), custom_call_target="InvertDiagBlocksLowerTriangular" | custom-call | tf_op jit(solution)/shard_map/triangular_solve/custom-call.0 | solution.py:29
  584.7 72.0 %custom-call.29 = f32[6,128,128]{2,1,0:T(8,128)} custom-call(f32[6,128,128]{2,1,0:T(8,128)} %slice.122), custom_call_target="Cholesky" | custom-call | tf_op jit(solution)/shard_map/cholesky/custom-call.2 | solution.py:28
  658.4 60.4 %custom-call.30 = f32[6,1,128,128]{2,3,1,0:T(8,128)} custom-call(f32[6,1,128,128]{3,2,1,0:T(8,128)} %select_bitcast_fusion.2), custom_call_target="InvertDiagBlocksLowerTriangular" | custom-call | tf_op jit(solution)/shard_map/cholesky/custom-call.4 | solution.py:28
  727.6 72.0 %custom-call.31 = f32[6,128,128]{2,1,0:T(8,128)} custom-call(f32[6,128,128]{2,1,0:T(8,128)} %convolution_subtract_fusion.6), custom_call_target="Cholesky" | custom-call | tf_op jit(solution)/shard_map/cholesky/custom-call.3 | solution.py:28
  807.3 7.7 while.9
  814.9 119.3 %custom-call.32 = f32[6,2,128,128]{2,3,1,0:T(8,128)} custom-call(f32[6,2,128,128]{3,2,1,0:T(8,128)} %bitcast.184), custom_call_target="InvertDiagBlocksLowerTriangular" | custom-call | tf_op jit(solution)/shard_map/triangular_solve/custom-call.0 | solution.py:29
  952.3 72.2 %custom-call.33 = f32[6,128,128]{2,1,0:T(8,128)} custom-call(f32[6,128,128]{2,1,0:T(8,128)} %slice.130), custom_call_target="Cholesky" | custom-call | tf_op jit(solution)/shard_map/cholesky/custom-call.2 | solution.py:28
  1026.3 60.4 %custom-call.34 = f32[6,1,128,128]{2,3,1,0:T(8,128)} custom-call(f32[6,1,128,128]{3,2,1,0:T(8,128)} %select_bitcast_fusion.1), custom_call_target="InvertDiagBlocksLowerTriangular" | custom-call | tf_op jit(solution)/shard_map/cholesky/custom-call.4 | solution.py:28
  1095.4 71.9 %custom-call.35 = f32[6,128,128]{2,1,0:T(8,128)} custom-call(f32[6,128,128]{2,1,0:T(8,128)} %convolution_subtract_fusion.5), custom_call_target="Cholesky" | custom-call | tf_op jit(solution)/shard_map/cholesky/custom-call.3 | solution.py:28
  1175.1 7.7 while.10
  1182.8 119.3 %custom-call.36 = f32[6,2,128,128]{2,3,1,0:T(8,128)} custom-call(f32[6,2,128,128]{3,2,1,0:T(8,128)} %bitcast.185), custom_call_target="InvertDiagBlocksLowerTriangular" | custom-call | tf_op jit(solution)/shard_map/triangular_solve/custom-call.0 | solution.py:29
  1316.4 70.6 %custom-call.37 = f32[6,128,128]{2,1,0:T(8,128)S(1)} custom-call(f32[6,128,128]{2,1,0:T(8,128)S(1)} %slice.138), custom_call_target="Cholesky" | custom-call | tf_op jit(solution)/shard_map/cholesky/custom-call.2 | solution.py:28
  1387.7 59.0 %custom-call.38 = f32[6,1,128,128]{2,3,1,0:T(8,128)S(1)} custom-call(f32[6,1,128,128]{3,2,1,0:T(8,128)S(1)} %select_bitcast_fusion), custom_call_target="InvertDiagBlocksLowerTriangular" | custom-call | tf_op jit(solution)/shard_map/cholesky/custom-call.4 | solution.py:28
  1452.1 72.0 %custom-call.39 = f32[6,128,128]{2,1,0:T(8,128)} custom-call(f32[6,128,128]{2,1,0:T(8,128)} %convolution_subtract_fusion.4), custom_call_target="Cholesky" | custom-call | tf_op jit(solution)/shard_map/cholesky/custom-call.3 | solution.py:28
  1535.8 119.3 %custom-call.40 = f32[6,2,128,128]{2,3,1,0:T(8,128)} custom-call(f32[6,2,128,128]{3,2,1,0:T(8,128)} %bitcast.182), custom_call_target="InvertDiagBlocksLowerTriangular" | custom-call | tf_op jit(solution)/shard_map/triangular_solve/custom-call.0 | solution.py:29
  1660.3 45.9 %all-gather.2.cloned.1.call-done = f32[24,256,256]{2,1,0:T(8,128)} async-done(((f32[6,256,256]{2,1,0:T(8,128)}), f32[24,256,256]{2,1,0:T(8,128)}) %all-gather.2.cloned.1.call-update) | async-done | bytes 6291472 | tf_op jit(solution)/shard_map/all_gather | solution.py:78
  1706.2 6.4 gather_fusion.1
  1712.6 6.3 broadcast_select_fusion
  (186 shorter events, 206.0 us)
Async XLA Ops:
  6.5 3.5 copy-start.16
  11.2 1.4 copy-start.18
  31.0 76.6 %all-to-all-start = ((f32[4,6,256,256]{3,2,1,0:T(8,128)}), f32[4,6,256,256]{3,2,1,0:T(8,128)}, u32[]{:S(2)}, u32[]{:S(2)}) async-start(f32[4,6,256,256]{3,2,1,0:T(8,128)} %broadcast_select_fusion.1), calls=%async_computation | async-start | bytes 12582912 | tf_op jit(solution)/shard_map/all_to_all | solution.py:50
  36.3 166.1 %all-reduce.3.cloned.1.call-start = ((), (), s32[]{:S(2)}) async-start(), calls=%async_computation.1 | async-start | bytes 3145728 | tf_op jit(solution)/shard_map/psum | solution.py:70
  112.2 1594.0 %all-gather.2.cloned.1.call-start = ((), (), s32[]{:S(2)}) async-start(), calls=%async_computation.2 | async-start | bytes 7864320 | tf_op jit(solution)/shard_map/all_gather | solution.py:78
  112.9 1194.5 %copy-start.19 = (pred[6]{0:T(512)(128)(4,1)}, pred[6]{0:T(512)(128)(4,1)S(1)}, u32[]{:S(2)}) copy-start(pred[6]{0:T(512)(128)(4,1)S(1)} %compare_bitcast_fusion) | copy-start | bytes 22
  113.0 911.6 %copy-start.15 = (pred[128,128]{1,0:T(8,128)(4,1)}, pred[128,128]{1,0:T(8,128)(4,1)S(1)}, u32[]{:S(2)}) copy-start(pred[128,128]{1,0:T(8,128)(4,1)S(1)} %iota_compare_fusion.3) | copy-start | bytes 49156
  113.1 1058.2 %copy-start.9 = (pred[256,256]{1,0:T(8,128)(4,1)}, pred[256,256]{1,0:T(8,128)(4,1)S(1)}, u32[]{:S(2)}) copy-start(pred[256,256]{1,0:T(8,128)(4,1)S(1)} %iota_compare_fusion) | copy-start | bytes 196612
  202.4 1.9 copy-start
  215.0 1.1 copy-start.3
  355.6 2.9 copy-start.6
  568.5 2.6 copy-start.11
  582.8 1.1 copy-start.4
  723.4 2.9 copy-start.7
  936.1 2.6 copy-start.12
  950.4 1.1 copy-start.5
  1091.3 2.9 copy-start.8
  1182.8 123.8 %copy-start.22 = (s32[2,2]{1,0:T(2,128)}, s32[2,2]{1,0:T(2,128)S(1)}, u32[]{:S(2)}) copy-start(s32[2,2]{1,0:T(2,128)S(1)} %get-tuple-element.285) | copy-start | bytes 52
  1304.0 2.6 copy-start.13
  1315.2 1.1 copy-start.2
  1524.1 3.3 copy-start.10
  1526.3 1.1 copy-start.1
  1527.4 2.6 copy-start.23
  1660.3 52.3 %copy-start.21 = (pred[4,6]{1,0:T(4,128)(4,1)S(1)}, pred[4,6]{1,0:T(4,128)(4,1)}, u32[]{:S(2)}) copy-start(pred[4,6]{1,0:T(4,128)(4,1)} %get-tuple-element.89) | copy-start | bytes 76
  (3 other events, 2.9 us)
Sparse Core Ops, SparseCore 0:
  112.3 90.0 all-reduce.2
  1660.4 45.7 all-gather.1
where the time goes:
time: 1740 us; the launch traced here: 1730 us
  other arithmetic  1350 us (78%)
  waiting for transfers between devices  207 us (12%)
  local copies, waits for them, and re-layouts  83.3 us (5%)
  matrix products  65.3 us (4%)
    another operation x33, other arithmetic, orthogonal_steps(): lower_factor = lax.linalg.cholesky(inner_gram)  829 us
    another operation x10, other arithmetic, orthogonal_steps(): lax.linalg.triangular_solve(lower_factor, projected, left_side=False, low...  487 us
    psum x1, waiting for transfers between devices, per_device(): lax.psum(route(stacked, owner_table, member, per_holder, per_factor), 'dp')  89.3 us
    all_to_all x1, waiting for transfers between devices, route(): lax.all_to_all(outgoing, 'work', split_axis=0, concat_axis=0, tiled=True)  71.3 us
    all_gather x1, waiting for transfers between devices, per_device(): all_bases = lax.all_gather(eigen_basis, 'work', axis=0, tiled=True)  45.9 us
  transfers between devices with their start and end apart: 3, of which 3 were waited for; matrix products, arithmetic and copies ran while one was open for 0% of the time, Pallas kernels for 0%

commit v1 on v0

v1 whole, which is shorter than its diff:
```python
import functools
import math

import jax
import jax.numpy as jnp
from jax import lax
from jax.experimental import pallas as pl
from jax.experimental.pallas import tpu as pltpu
from jax.sharding import PartitionSpec as P

BS = 256
HB = 128
ITERS = 4
DAMPING = 0.1
HI = lax.Precision.HIGHEST


def dot(a, b, ca, cb, precision=HI):
    return lax.dot_general(
        a, b, (((ca,), (cb,)), ((), ())), precision=precision, preferred_element_type=jnp.float32
    )


def inv_chol(s):
    n=HB
    row=lax.broadcasted_iota(jnp.int32,(n,n),0); col=lax.broadcasted_iota(jnp.int32,(n,n),1)
    eye=row==col
    diag=jnp.where(eye,s,0.0)
    drow=lax.rsqrt(jnp.sum(diag,axis=0,keepdims=True)); dcol=lax.rsqrt(jnp.sum(diag,axis=1,keepdims=True))
    s=s*drow*dcol
    w=[s[8*g:8*g+8,:] for g in range(n//8)]
    lane=lax.broadcasted_iota(jnp.int32,(8,n),1); sub=lax.broadcasted_iota(jnp.int32,(8,n),0)
    for j in range(n):
        g0,t=divmod(j,8)
        r=jnp.broadcast_to(w[g0][t:t+1,:],(8,n))
        p=jnp.broadcast_to(r[:,j:j+1],(8,n))
        inv=1.0/p
        rr=jnp.where(lane==j,1.0+inv,r*inv)
        for g in range(g0,n//8):
            if g==g0 and t==7: continue
            c=jnp.broadcast_to(w[g][:,j:j+1],(8,n))
            if g==g0: c=jnp.where(sub>t,c,0.0)
            w[g]=w[g]-c*rr
    w=jnp.concatenate(w,axis=0)
    d=lax.rsqrt(jnp.sum(jnp.where(eye,w,0.0),axis=1,keepdims=True))
    return jnp.where(col<row,w,jnp.where(eye,1.0,0.0))*d*drow

def basis_body(x_ref,tokens,f_ref,y_ref,q_ref):
    x=x_ref[...].astype(jnp.bfloat16)
    g=lax.dot_general(x,x,(((0,),(0,)),((),())),preferred_element_type=jnp.float32)*(1.0/tokens)
    row=lax.broadcasted_iota(jnp.int32,(BS,BS),0); col=lax.broadcasted_iota(jnp.int32,(BS,BS),1)
    eye=row==col
    tr=jnp.sum(jnp.sum(jnp.where(eye,g,0.0),axis=0,keepdims=True),axis=1,keepdims=True)/BS
    f=g+jnp.where(eye,DAMPING*tr,0.0)
    f_ref[...]=f
    y_ref[...]=f
    def it(i,_):
        y1=y_ref[:,:HB]
        b1=inv_chol(dot(y1,y1,0,0))
        q1=dot(y1,b1,1,1)
        q_ref[:,:HB]=q1
        y2=y_ref[:,HB:]
        z2=y2-dot(q1,dot(q1,y2,0,0),1,0)
        b2=inv_chol(dot(z2,z2,0,0))
        q_ref[:,HB:]=dot(z2,b2,1,1)
        @pl.when(i<ITERS-1)
        def _():
            y_ref[...]=dot(f_ref[...],q_ref[...],1,0)
        return 0
    lax.fori_loop(0,ITERS,it,0)


def pick_kernel(per_holder, per_factor, slots, table_ref, *refs):
    sources, out_ref, held, sems = refs[:4], refs[4], refs[5], refs[6]
    member = lax.axis_index("work")
    owners, per_owner = table_ref.shape

    def locate(i):
        b = table_ref[i // per_owner, i % per_owner]
        within = b % per_factor
        mine = (b >= 0) & (within // per_holder == member)
        return b // per_factor, within % per_holder, mine

    def begin(i, count):
        source, k, mine = locate(i)
        for f in range(4):

            @pl.when(mine & (source == f))
            def _():
                cols = pl.ds(pl.multiple_of(k * BS, BS), BS)
                slot = jnp.minimum(count, slots - 1)
                pltpu.make_async_copy(sources[f].at[:, cols], held.at[slot], sems.at[slot]).start()

        return count + jnp.where(mine, 1, 0)

    count = lax.fori_loop(0, owners * per_owner, begin, 0)
    for j in range(out_ref.shape[0]):
        if j >= slots:
            out_ref[j] = jnp.zeros(out_ref.shape[1:], jnp.float32)
            continue

        @pl.when(j < count)
        def _():
            pltpu.make_async_copy(sources[0].at[:, pl.ds(0, BS)], held.at[j], sems.at[j]).wait()
            out_ref[j] = held[j].astype(jnp.float32)

        @pl.when(j >= count)
        def _():
            out_ref[j] = jnp.zeros(out_ref.shape[1:], jnp.float32)


def pick(table, sources, per_holder, per_factor, slots, places):
    rows = sources[0].shape[0]
    return pl.pallas_call(
        functools.partial(pick_kernel, per_holder, per_factor, slots),
        out_shape=jax.ShapeDtypeStruct((places, rows, BS), jnp.float32),
        in_specs=[pl.BlockSpec(memory_space=pltpu.SMEM)] + [pl.BlockSpec(memory_space=pl.ANY)] * 4,
        out_specs=pl.BlockSpec(memory_space=pltpu.VMEM),
        scratch_shapes=[
            pltpu.VMEM((slots, rows, BS), jnp.bfloat16),
            pltpu.SemaphoreType.DMA((slots,)),
        ],
        compiler_params=pltpu.CompilerParams(vmem_limit_bytes=48 << 20),
    )(table, *sources)


def place_kernel(per_holder, per_factor, workers, table_ref, bases_ref, out_ref, zeros, counts, sems):
    owners, per_owner = table_ref.shape
    zeros[...] = jnp.zeros_like(zeros)
    for h in range(workers):
        counts[h] = 0

    def begin(i, carry):
        b = table_ref[i // per_owner, i % per_owner]

        @pl.when(b >= 0)
        def _():
            holder = b % per_factor // per_holder
            nth = counts[holder]
            counts[holder] = nth + 1
            pltpu.make_async_copy(
                bases_ref.at[nth * workers + holder], out_ref.at[i], sems.at[i]
            ).start()

        @pl.when(b < 0)
        def _():
            pltpu.make_async_copy(zeros, out_ref.at[i], sems.at[i]).start()

        return carry

    lax.fori_loop(0, owners * per_owner, begin, 0)

    def end(i, carry):
        pltpu.make_async_copy(zeros, out_ref.at[i], sems.at[i]).wait()
        return carry

    lax.fori_loop(0, owners * per_owner, end, 0)


def place(table, bases, per_holder, per_factor, workers):
    flat = table.shape[0] * table.shape[1]
    return pl.pallas_call(
        functools.partial(place_kernel, per_holder, per_factor, workers),
        out_shape=jax.ShapeDtypeStruct((flat, BS, BS), jnp.float32),
        in_specs=[pl.BlockSpec(memory_space=pltpu.SMEM), pl.BlockSpec(memory_space=pl.ANY)],
        out_specs=pl.BlockSpec(memory_space=pl.ANY),
        scratch_shapes=[
            pltpu.VMEM((BS, BS), jnp.float32),
            pltpu.SMEM((workers,), jnp.int32),
            pltpu.SemaphoreType.DMA((flat,)),
        ],
    )(table, bases)


def basis_kernel(x_ref, o_ref, f_ref, y_ref):
    basis_body(x_ref, x_ref.shape[0], f_ref, y_ref, o_ref)
    o_ref[...] = o_ref[...] * math.sqrt(BS)


def basis(x):
    return pl.pallas_call(
        basis_kernel,
        out_shape=jax.ShapeDtypeStruct((BS, BS), jnp.float32),
        scratch_shapes=[pltpu.VMEM((BS, BS), jnp.float32)] * 2,
        compiler_params=pltpu.CompilerParams(vmem_limit_bytes=48 << 20),
    )(x)


def per_device(act_one, grad_one, act_two, grad_two, owner_table):
    workers = lax.axis_size("work")
    replicas = lax.axis_size("dp")
    tok_rows, feature_width = act_one.shape
    per_holder = feature_width // BS
    per_factor = per_holder * workers
    slots = owner_table.shape[1]
    span = next(n for n in range(slots, replicas + 1) if replicas % n == 0)
    picked = pick(
        owner_table, (act_one, grad_one, act_two, grad_two), per_holder, per_factor, slots, span
    )
    picked = jnp.tile(picked, (replicas // span, 1, 1))
    mine = lax.all_to_all(picked, "dp", split_axis=0, concat_axis=0, tiled=True)
    base = basis(mine.reshape(replicas * tok_rows, BS))
    groups = None
    if span < replicas:
        each = span * workers
        groups = [list(range(i, i + each)) for i in range(0, replicas * workers, each)]
    bases = lax.all_gather(base, ("dp", "work"), axis=0, tiled=False, axis_index_groups=groups)
    placed = place(owner_table, bases, per_holder, per_factor, workers)
    return placed.reshape(workers, slots, BS, BS)


def solution(mesh):
    in_specs = (P("dp", "work"), P("dp", "work"), P("dp", "work"), P("dp", "work"), P())
    return jax.shard_map(
        per_device, mesh=mesh, in_specs=in_specs, out_specs=P(), check_vma=False
    )
```

time: 1740 us -> 376 us (0.22)
  other arithmetic: 1350 us -> 0 us
  Pallas kernels: 0 us -> 249 us
  waiting for transfers between devices: 207 us -> 76.8 us
  local copies, waits for them, and re-layouts: 83.3 us -> 4.57 us
  matrix products: 65.3 us -> 0 us
  blocking collectives: 0 us -> 32.8 us
    another operation x43 -> x0, other arithmetic: 1320 us -> none  [the longest x33 829 us: orthogonal_steps(): lower_factor = lax.linalg.cholesky(inner_gram)]
    pallas_call x0 -> x3, Pallas kernels: none -> 249 us  [the longest x1 149 us: basis(): pl.pallas_call(basis_kernel, out_shape=jax.ShapeDtypeStruct((BS, BS), jnp...]
    psum x1 -> x0, waiting for transfers between devices: 89.3 us -> none  [per_device(): lax.psum(route(stacked, owner_table, member, per_holder, per_factor), 'dp')]
    all_to_all x1 -> x0, waiting for transfers between devices: 71.3 us -> none  [route(): lax.all_to_all(outgoing, 'work', split_axis=0, concat_axis=0, tiled=True)]
    another operation x41 -> x0, local copies, waits for them, and re-layouts: 48 us -> none  [the longest x29 32.6 us: orthogonal_steps(): lax.linalg.triangular_solve(lower_factor, projected, left_side=False, low...]
    another operation x20 -> x0, matrix products: 40.4 us -> none  [the longest x8 21 us: orthogonal_steps(): lower_factor = lax.linalg.cholesky(inner_gram)]
    all_to_all x0 -> x1, blocking collectives: none -> 32.8 us  [per_device(): mine = lax.all_to_all(picked, 'dp', split_axis=0, concat_axis=0, tiled=True)]
    all_gather x1, waiting for transfers between devices: 45.9 us -> 76.7 us  [per_device(): lax.all_gather(base, ('dp', 'work'), axis=0, tiled=False, axis_index_grou...]
  transfers between devices with their start and end apart: 3 -> 1, of which waited for: 3 -> 1; matrix products, arithmetic and copies ran while one was open for 0% -> 0% of each run, Pallas kernels for 0% -> 0%
where the time goes in v1:
time: 376 us
  Pallas kernels  249 us (66%)
  waiting for transfers between devices  76.8 us (20%)
  blocking collectives  32.8 us (9%)
  between operations  13.4 us (4%)
  local copies, waits for them, and re-layouts  4.57 us (1%)
    pallas_call x1, Pallas kernels, basis(): pl.pallas_call(basis_kernel, out_shape=jax.ShapeDtypeStruct((BS, BS), jnp...  149 us
    pallas_call x1, Pallas kernels, place(): pl.pallas_call(functools.partial(place_kernel, per_holder, per_factor, wo...  97.5 us
    all_gather x1, waiting for transfers between devices, per_device(): lax.all_gather(base, ('dp', 'work'), axis=0, tiled=False, axis_index_grou...  76.7 us
    all_to_all x1, blocking collectives, per_device(): mine = lax.all_to_all(picked, 'dp', split_axis=0, concat_axis=0, tiled=True)  32.8 us
  transfers between devices with their start and end apart: 1, of which 1 were waited for; matrix products, arithmetic and copies ran while one was open for 0% of the time, Pallas kernels for 0%

profile of v1, /device:TPU:0, one launch (start us, length us, event | category | flops | bytes accessed | tf_op | source)
XLA Modules:
  0.0 376.2 jit_solution(18100741791710323367)
XLA Ops:
  6.5 0.0 all-gather.3.cloned.1.call-start
  6.5 0.0 copy-start
  6.5 1.0 copy-done
  7.5 0.0 copy-start.1
  7.5 1.0 copy-done.1
  8.5 0.0 copy-start.2
  8.5 1.0 copy-done.2
  9.5 0.0 copy-start.3
  9.5 1.0 copy-done.3
  10.4 0.0 copy-start.4
  10.4 0.7 copy-done.4
  11.1 2.3 shard_map.55
  13.4 32.8 %all_to_all.5 = f32[8,128,256]{2,1,0:T(8,128)S(1)} all-to-all(f32[8,128,256]{2,1,0:T(8,128)S(1)} %shard_map.55), channel_id=1, replica_groups=mesh['dp'=8,'work'=4] {'dp'}, dimensions={0} | all-to-all | bytes 2097152 | tf_op jit(solution)/shard_map/all_to_all | solution.py:201
  46.2 148.8 %shard_map.56 = f32[256,256]{1,0:T(8,128)} custom-call(f32[1024,256]{1,0:T(8,128)S(1)} %bitcast.3), custom_call_target="tpu_custom_call" | custom-call | tf_op jit(solution)/shard_map/pallas_call | solution.py:181
  195.0 0.0 all-gather.3.cloned.1.call-update
  195.0 76.7 %all-gather.3.cloned.1.call-done = f32[8192,256]{1,0:T(8,128)} async-done(((f32[256,256]{1,0:T(8,128)}), f32[8192,256]{1,0:T(8,128)}) %all-gather.3.cloned.1.call-update) | async-done | bytes 8388624 | tf_op jit(solution)/shard_map/all_gather | solution.py:207
  271.8 97.5 %shard_map.57 = f32[24,256,256]{2,1,0:T(8,128)} custom-call(s32[4,6]{1,0:T(4,128)} %table_ref.3, f32[32,256,256]{2,1,0:T(8,128)} %bitcast.4), custom_call_target="tpu_custom_call" | custom-call | tf_op jit(solution)/shard_map/pallas_call | solution.py:162
Async XLA Ops:
  6.5 265.3 %all-gather.3.cloned.1.call-start = ((), (), s32[]{:S(2)}) async-start(), calls=%async_computation.1 | async-start | bytes 8650752 | tf_op jit(solution)/shard_map/all_gather | solution.py:207
  6.5 1.0 copy-start
  7.5 1.0 copy-start.1
  8.5 1.0 copy-start.2
  9.5 1.0 copy-start.3
  10.4 0.7 copy-start.4
Sparse Core Ops, SparseCore 0:
  195.2 76.5 all-gather.2

commit v2 on v1

--- a/solution.py
+++ b/solution.py
@@ -9,7 +9,7 @@
 from jax.sharding import PartitionSpec as P
 
 BS = 256
-HB = 128
+NB = 32
 ITERS = 4
 DAMPING = 0.1
 HI = lax.Precision.HIGHEST
@@ -21,53 +21,72 @@
     )
 
 
-def inv_chol(s):
-    n=HB
-    row=lax.broadcasted_iota(jnp.int32,(n,n),0); col=lax.broadcasted_iota(jnp.int32,(n,n),1)
-    eye=row==col
-    diag=jnp.where(eye,s,0.0)
-    drow=lax.rsqrt(jnp.sum(diag,axis=0,keepdims=True)); dcol=lax.rsqrt(jnp.sum(diag,axis=1,keepdims=True))
-    s=s*drow*dcol
-    w=[s[8*g:8*g+8,:] for g in range(n//8)]
-    lane=lax.broadcasted_iota(jnp.int32,(8,n),1); sub=lax.broadcasted_iota(jnp.int32,(8,n),0)
+def eliminate(mats, n):
+    row = lax.broadcasted_iota(jnp.int32, (n, n), 0)
+    col = lax.broadcasted_iota(jnp.int32, (n, n), 1)
+    eye = row == col
+    lane = lax.broadcasted_iota(jnp.int32, (8, n), 1)
+    sub = lax.broadcasted_iota(jnp.int32, (8, n), 0)
+    scales, works = [], []
+    for s in mats:
+        diag = jnp.where(eye, s, 0.0)
+        down = lax.rsqrt(jnp.sum(diag, axis=0, keepdims=True))
+        across = lax.rsqrt(jnp.sum(diag, axis=1, keepdims=True))
+        s = s * down * across
+        scales.append(down)
+        works.append([s[8 * g : 8 * g + 8, :] for g in range(n // 8)])
     for j in range(n):
-        g0,t=divmod(j,8)
-        r=jnp.broadcast_to(w[g0][t:t+1,:],(8,n))
-        p=jnp.broadcast_to(r[:,j:j+1],(8,n))
-        inv=1.0/p
-        rr=jnp.where(lane==j,1.0+inv,r*inv)
-        for g in range(g0,n//8):
-            if g==g0 and t==7: continue
-            c=jnp.broadcast_to(w[g][:,j:j+1],(8,n))
-            if g==g0: c=jnp.where(sub>t,c,0.0)
-            w[g]=w[g]-c*rr
-    w=jnp.concatenate(w,axis=0)
-    d=lax.rsqrt(jnp.sum(jnp.where(eye,w,0.0),axis=1,keepdims=True))
-    return jnp.where(col<row,w,jnp.where(eye,1.0,0.0))*d*drow
-
-def basis_body(x_ref,tokens,f_ref,y_ref,q_ref):
-    x=x_ref[...].astype(jnp.bfloat16)
-    g=lax.dot_general(x,x,(((0,),(0,)),((),())),preferred_element_type=jnp.float32)*(1.0/tokens)
-    row=lax.broadcasted_iota(jnp.int32,(BS,BS),0); col=lax.broadcasted_iota(jnp.int32,(BS,BS),1)
-    eye=row==col
-    tr=jnp.sum(jnp.sum(jnp.where(eye,g,0.0),axis=0,keepdims=True),axis=1,keepdims=True)/BS
-    f=g+jnp.where(eye,DAMPING*tr,0.0)
-    f_ref[...]=f
-    y_ref[...]=f
-    def it(i,_):
-        y1=y_ref[:,:HB]
-        b1=inv_chol(dot(y1,y1,0,0))
-        q1=dot(y1,b1,1,1)
-        q_ref[:,:HB]=q1
-        y2=y_ref[:,HB:]
-        z2=y2-dot(q1,dot(q1,y2,0,0),1,0)
-        b2=inv_chol(dot(z2,z2,0,0))
-        q_ref[:,HB:]=dot(z2,b2,1,1)
-        @pl.when(i<ITERS-1)
-        def _():
-            y_ref[...]=dot(f_ref[...],q_ref[...],1,0)
-        return 0
-    lax.fori_loop(0,ITERS,it,0)
+        first, t = divmod(j, 8)
+        for w in works:
+            pivot = jnp.broadcast_to(w[first][:, j : j + 1], (8, n))
+            inverse = 1.0 / pivot
+            scaled = jnp.where(lane == j, 1.0 + inverse, w[first] * inverse)
+            scaled = jnp.broadcast_to(scaled[t : t + 1, :], (8, n))
+            for g in range(first, n // 8):
+                if g == first:
+                    if t < 7:
+                        w[g] = w[g] - jnp.where(sub > t, pivot, 0.0) * scaled
+                else:
+                    w[g] = w[g] - jnp.broadcast_to(w[g][:, j : j + 1], (8, n)) * scaled
+    found = []
+    for w, down in zip(works, scales):
+        w = jnp.concatenate(w, axis=0)
+        d = lax.rsqrt(jnp.sum(jnp.where(eye, w, 0.0), axis=1, keepdims=True))
+        found.append(jnp.where(col < row, w, jnp.where(eye, 1.0, 0.0)) * d * down)
+    return found
+
+
+def basis_body(x_ref, f_ref, q_ref):
+    x = x_ref[...].astype(jnp.bfloat16)
+    g = lax.dot_general(x, x, (((0,), (0,)), ((), ())), preferred_element_type=jnp.float32)
+    g = g * (1.0 / x_ref.shape[0])
+    row = lax.broadcasted_iota(jnp.int32, (BS, BS), 0)
+    col = lax.broadcasted_iota(jnp.int32, (BS, BS), 1)
+    eye = row == col
+    trace = jnp.sum(
+        jnp.sum(jnp.where(eye, g, 0.0), axis=0, keepdims=True), axis=1, keepdims=True
+    )
+    f_ref[...] = g + jnp.where(eye, DAMPING / BS * trace, 0.0)
+    for stage in range(ITERS + BS // NB - 1):
+        active = [(k, stage - k) for k in range(ITERS) if 0 <= stage - k < BS // NB]
+        span = {b: slice(b * NB, b * NB + NB) for _, b in active}
+        later = [(k, b) for k, b in active if k > 0]
+        moved = {}
+        if later:
+            held = [q_ref[k - 1, span[b], :] for k, b in later]
+            held = jnp.concatenate(held, axis=0) if len(held) > 1 else held[0]
+            product = dot(held, f_ref[...], 1, 0)
+            moved = {kb: product[i * NB : i * NB + NB] for i, kb in enumerate(later)}
+        rests = []
+        for k, b in active:
+            y = moved[(k, b)] if k else f_ref[span[b], :]
+            if b:
+                before = q_ref[k, : b * NB, :]
+                y = y - dot(dot(y, before, 1, 1), before, 1, 0)
+            rests.append(y)
+        factors = eliminate([dot(z, z, 1, 1) for z in rests], NB)
+        for (k, b), z, t in zip(active, rests, factors):
+            q_ref[k, span[b], :] = dot(t, z, 1, 0)
 
 
 def pick_kernel(per_holder, per_factor, slots, table_ref, *refs):
@@ -124,9 +143,9 @@
     )(table, *sources)
 
 
-def place_kernel(per_holder, per_factor, workers, table_ref, bases_ref, out_ref, zeros, counts, sems):
+def place_kernel(per_holder, per_factor, workers, table_ref, bases_ref, out_ref, held, zeros, counts, sems):
     owners, per_owner = table_ref.shape
-    zeros[...] = jnp.zeros_like(zeros)
+    flat = owners * per_owner
     for h in range(workers):
         counts[h] = 0
 
@@ -139,22 +158,38 @@
             nth = counts[holder]
             counts[holder] = nth + 1
             pltpu.make_async_copy(
-                bases_ref.at[nth * workers + holder], out_ref.at[i], sems.at[i]
+                bases_ref.at[nth * workers + holder], held.at[i], sems.at[0, i]
             ).start()
 
-        @pl.when(b < 0)
-        def _():
-            pltpu.make_async_copy(zeros, out_ref.at[i], sems.at[i]).start()
-
-        return carry
-
-    lax.fori_loop(0, owners * per_owner, begin, 0)
+        return carry
+
+    lax.fori_loop(0, flat, begin, 0)
+    zeros[...] = jnp.zeros_like(zeros)
+
+    def empty(i, carry):
+        @pl.when(table_ref[i // per_owner, i % per_owner] < 0)
+        def _():
+            pltpu.make_async_copy(zeros, out_ref.at[i], sems.at[1, i]).start()
+
+        return carry
+
+    lax.fori_loop(0, flat, empty, 0)
+
+    def forward(i, carry):
+        @pl.when(table_ref[i // per_owner, i % per_owner] >= 0)
+        def _():
+            pltpu.make_async_copy(bases_ref.at[0], held.at[i], sems.at[0, i]).wait()
+            pltpu.make_async_copy(held.at[i], out_ref.at[i], sems.at[1, i]).start()
+
+        return carry
+
+    lax.fori_loop(0, flat, forward, 0)
 
     def end(i, carry):
-        pltpu.make_async_copy(zeros, out_ref.at[i], sems.at[i]).wait()
-        return carry
-
-    lax.fori_loop(0, owners * per_owner, end, 0)
+        pltpu.make_async_copy(zeros, out_ref.at[i], sems.at[1, i]).wait()
+        return carry
+
+    lax.fori_loop(0, flat, end, 0)
 
 
 def place(table, bases, per_holder, per_factor, workers):
@@ -165,23 +200,28 @@
         in_specs=[pl.BlockSpec(memory_space=pltpu.SMEM), pl.BlockSpec(memory_space=pl.ANY)],
         out_specs=pl.BlockSpec(memory_space=pl.ANY),
         scratch_shapes=[
+            pltpu.VMEM((flat, BS, BS), jnp.float32),
             pltpu.VMEM((BS, BS), jnp.float32),
             pltpu.SMEM((workers,), jnp.int32),
-            pltpu.SemaphoreType.DMA((flat,)),
+            pltpu.SemaphoreType.DMA((2, flat)),
         ],
+        compiler_params=pltpu.CompilerParams(vmem_limit_bytes=48 << 20),
     )(table, bases)
 
 
-def basis_kernel(x_ref, o_ref, f_ref, y_ref):
-    basis_body(x_ref, x_ref.shape[0], f_ref, y_ref, o_ref)
-    o_ref[...] = o_ref[...] * math.sqrt(BS)
+def basis_kernel(x_ref, o_ref, f_ref, q_ref):
+    basis_body(x_ref, f_ref, q_ref)
+    o_ref[...] = q_ref[ITERS - 1].T * math.sqrt(BS)
 
 
 def basis(x):
     return pl.pallas_call(
         basis_kernel,
         out_shape=jax.ShapeDtypeStruct((BS, BS), jnp.float32),
-        scratch_shapes=[pltpu.VMEM((BS, BS), jnp.float32)] * 2,
+        scratch_shapes=[
+            pltpu.VMEM((BS, BS), jnp.float32),
+            pltpu.VMEM((ITERS, BS, BS), jnp.float32),
+        ],
         compiler_params=pltpu.CompilerParams(vmem_limit_bytes=48 << 20),
     )(x)
 

time: 376 us -> 184 us (0.49)
  Pallas kernels: 249 us -> 54.9 us
    pallas_call x1, Pallas kernels: 149 us -> 48 us  [basis(): pl.pallas_call(basis_kernel, out_shape=jax.ShapeDtypeStruct((BS, BS), jnp...]
    pallas_call x1, Pallas kernels: 97.5 us -> 4.62 us  [place(): pl.pallas_call(functools.partial(place_kernel, per_holder, per_factor, wo...]
where the time goes in v2:
time: 184 us; the launch traced here: 183 us
  waiting for transfers between devices  76.8 us (42%)
  Pallas kernels  54.9 us (30%)
  blocking collectives  32.8 us (18%)
  between operations  13.4 us (7%)
  local copies, waits for them, and re-layouts  5.25 us (3%)
    all_gather x1, waiting for transfers between devices, per_device(): lax.all_gather(base, ('dp', 'work'), axis=0, tiled=False, axis_index_grou...  76.7 us
    pallas_call x1, Pallas kernels, basis(): pl.pallas_call(basis_kernel, out_shape=jax.ShapeDtypeStruct((BS, BS), jnp...  48 us
    all_to_all x1, blocking collectives, per_device(): mine = lax.all_to_all(picked, 'dp', split_axis=0, concat_axis=0, tiled=True)  32.8 us
    unnamed x12, local copies, waits for them, and re-layouts  5.25 us
    pallas_call x1, Pallas kernels, place(): pl.pallas_call(functools.partial(place_kernel, per_holder, per_factor, wo...  4.62 us
  transfers between devices with their start and end apart: 1, of which 1 were waited for; matrix products, arithmetic and copies ran while one was open for 0% of the time, Pallas kernels for 0%

profile of v2, /device:TPU:0, one launch (start us, length us, event | category | flops | bytes accessed | tf_op | source)
XLA Modules:
  0.0 183.1 jit_solution(3838917674030085739)
XLA Ops:
  6.5 0.0 all-gather.3.cloned.1.call-start
  6.5 0.0 copy-start
  6.5 1.0 copy-done
  7.5 0.0 copy-start.1
  7.5 1.0 copy-done.1
  8.5 0.0 copy-start.2
  8.5 1.0 copy-done.2
  9.5 0.0 copy-start.3
  9.5 1.0 copy-done.3
  10.4 0.0 copy-start.4
  10.4 0.7 copy-done.4
  11.1 2.3 %shard_map.55 = f32[8,128,256]{2,1,0:T(8,128)S(1)} custom-call(s32[4,6]{1,0:T(4,128)S(1)} %copy-done.4, bf16[128,1280]{1,0:T(8,128)(2,1)S(1)} %copy-done, bf16[128,1280]{1,0:T(8,128)(2,1)S(1)} %copy-done.1, bf16[128,1280]{1,0:T(8,128)(2,1)S(1)} %copy-done.2, bf16[128,1280]{1,0:T(8,128)(2,1)S(1)} %copy-done.3), custom_call_target="tpu_custom_call" | custom-call | tf_op jit(solution)/shard_map/pallas_call | solution.py:133
  13.5 32.8 %all_to_all.5 = f32[8,128,256]{2,1,0:T(8,128)S(1)} all-to-all(f32[8,128,256]{2,1,0:T(8,128)S(1)} %shard_map.55), channel_id=1, replica_groups=mesh['dp'=8,'work'=4] {'dp'}, dimensions={0} | all-to-all | bytes 2097152 | tf_op jit(solution)/shard_map/all_to_all | solution.py:241
  46.2 48.0 %shard_map.56 = f32[256,256]{1,0:T(8,128)} custom-call(f32[1024,256]{1,0:T(8,128)S(1)} %bitcast.3), custom_call_target="tpu_custom_call" | custom-call | tf_op jit(solution)/shard_map/pallas_call | solution.py:218
  94.2 0.0 all-gather.3.cloned.1.call-update
  94.2 76.7 %all-gather.3.cloned.1.call-done = f32[8192,256]{1,0:T(8,128)} async-done(((f32[256,256]{1,0:T(8,128)}), f32[8192,256]{1,0:T(8,128)}) %all-gather.3.cloned.1.call-update) | async-done | bytes 8388624 | tf_op jit(solution)/shard_map/all_gather | solution.py:247
  171.0 0.0 copy-start.5
  171.0 0.7 copy-done.5
  171.7 4.6 %shard_map.57 = f32[24,256,256]{2,1,0:T(8,128)} custom-call(s32[4,6]{1,0:T(4,128)S(1)} %copy-done.5, f32[32,256,256]{2,1,0:T(8,128)} %bitcast.4), custom_call_target="tpu_custom_call" | custom-call | tf_op jit(solution)/shard_map/pallas_call | solution.py:197
Async XLA Ops:
  6.5 164.4 %all-gather.3.cloned.1.call-start = ((), (), s32[]{:S(2)}) async-start(), calls=%async_computation.1 | async-start | bytes 8650752 | tf_op jit(solution)/shard_map/all_gather | solution.py:247
  6.5 1.0 copy-start
  7.5 1.0 copy-start.1
  8.5 1.0 copy-start.2
  9.5 1.0 copy-start.3
  10.4 0.7 copy-start.4
  171.0 0.7 copy-start.5
Sparse Core Ops, SparseCore 0:
  94.4 76.5 all-gather.2

commit v3 on v2

--- a/solution.py
+++ b/solution.py
@@ -143,6 +143,77 @@
     )(table, *sources)
 
 
+def exchange_kernel(replicas, span, slots, picked_ref, out_ref, send_sems, recv_sems, own_sem):
+    me = lax.axis_index("dp")
+    barrier = pltpu.get_barrier_semaphore()
+
+    def greet(d, carry):
+        pl.semaphore_signal(
+            barrier, inc=1, device_id={"dp": (me + d) % replicas}, device_id_type=pl.DeviceIdType.MESH
+        )
+        return carry
+
+    lax.fori_loop(1, replicas, greet, 0)
+    pl.semaphore_wait(barrier, replicas - 1)
+
+    def copy(d):
+        target = (me + d) % replicas
+        return target % span < slots, pltpu.make_async_remote_copy(
+            src_ref=picked_ref.at[target % span],
+            dst_ref=out_ref.at[me],
+            send_sem=send_sems.at[d],
+            recv_sem=recv_sems.at[d],
+            device_id={"dp": target},
+            device_id_type=pl.DeviceIdType.MESH,
+        )
+
+    def begin(d, carry):
+        wanted, moving = copy(d)
+
+        @pl.when(wanted)
+        def _():
+            moving.start()
+
+        return carry
+
+    lax.fori_loop(1, replicas, begin, 0)
+    own = pltpu.make_async_copy(picked_ref.at[me % span], out_ref.at[me], own_sem)
+    own.start()
+    own.wait()
+
+    def end(d, carry):
+        wanted, moving = copy(d)
+
+        @pl.when(wanted)
+        def _():
+            moving.wait_send()
+
+        @pl.when(me % span < slots)
+        def _():
+            moving.wait_recv()
+
+        return carry
+
+    lax.fori_loop(1, replicas, end, 0)
+
+
+def exchange(picked, replicas, span, slots):
+    return pl.pallas_call(
+        functools.partial(exchange_kernel, replicas, span, slots),
+        out_shape=jax.ShapeDtypeStruct((replicas,) + picked.shape[1:], jnp.float32),
+        in_specs=[pl.BlockSpec(memory_space=pltpu.VMEM)],
+        out_specs=pl.BlockSpec(memory_space=pltpu.VMEM),
+        scratch_shapes=[
+            pltpu.SemaphoreType.DMA((replicas,)),
+            pltpu.SemaphoreType.DMA((replicas,)),
+            pltpu.SemaphoreType.DMA,
+        ],
+        compiler_params=pltpu.CompilerParams(
+            collective_id=0, has_side_effects=True, vmem_limit_bytes=48 << 20
+        ),
+    )(picked)
+
+
 def place_kernel(per_holder, per_factor, workers, table_ref, bases_ref, out_ref, held, zeros, counts, sems):
     owners, per_owner = table_ref.shape
     flat = owners * per_owner
@@ -237,8 +308,7 @@
     picked = pick(
         owner_table, (act_one, grad_one, act_two, grad_two), per_holder, per_factor, slots, span
     )
-    picked = jnp.tile(picked, (replicas // span, 1, 1))
-    mine = lax.all_to_all(picked, "dp", split_axis=0, concat_axis=0, tiled=True)
+    mine = exchange(picked, replicas, span, slots)
     base = basis(mine.reshape(replicas * tok_rows, BS))
     groups = None
     if span < replicas:

time: 184 us -> 180 us (0.978)
  blocking collectives: 32.8 us -> 0 us
  Pallas kernels: 54.9 us -> 76.7 us
  waiting for transfers between devices: 76.8 us -> 84.2 us
    all_to_all x1 -> x0, blocking collectives: 32.8 us -> none  [per_device(): mine = lax.all_to_all(picked, 'dp', split_axis=0, concat_axis=0, tiled=True)]
    pallas_call x0 -> x1, Pallas kernels: none -> 21.4 us  [exchange(): pl.pallas_call(functools.partial(exchange_kernel, replicas, span, slots),...]
    all_gather x1, waiting for transfers between devices: 76.7 us -> 84.2 us  [per_device(): lax.all_gather(base, ('dp', 'work'), axis=0, tiled=False, axis_index_grou...]
where the time goes in v3:
time: 180 us
  waiting for transfers between devices  84.2 us (47%)
  Pallas kernels  76.7 us (43%)
  between operations  13.4 us (7%)
  local copies, waits for them, and re-layouts  5.25 us (3%)
    all_gather x1, waiting for transfers between devices, per_device(): lax.all_gather(base, ('dp', 'work'), axis=0, tiled=False, axis_index_grou...  84.2 us
    pallas_call x1, Pallas kernels, basis(): pl.pallas_call(basis_kernel, out_shape=jax.ShapeDtypeStruct((BS, BS), jnp...  48 us
    pallas_call x1, Pallas kernels, exchange(): pl.pallas_call(functools.partial(exchange_kernel, replicas, span, slots),...  21.4 us
    unnamed x12, local copies, waits for them, and re-layouts  5.25 us
    pallas_call x1, Pallas kernels, place(): pl.pallas_call(functools.partial(place_kernel, per_holder, per_factor, wo...  5.03 us
  transfers between devices with their start and end apart: 1, of which 1 were waited for; matrix products, arithmetic and copies ran while one was open for 0% of the time, Pallas kernels for 0%

profile of v3, /device:TPU:0, one launch (start us, length us, event | category | flops | bytes accessed | tf_op | source)
XLA Modules:
  0.0 179.6 jit_solution(2164647698699191692)
XLA Ops:
  6.5 0.0 all-gather.3.cloned.1.call-start
  6.5 0.0 copy-start
  6.5 1.0 copy-done
  7.5 0.0 copy-start.1
  7.5 1.0 copy-done.1
  8.5 0.0 copy-start.2
  8.5 1.0 copy-done.2
  9.5 0.0 copy-start.3
  9.5 1.0 copy-done.3
  10.4 0.0 copy-start.4
  10.4 0.7 copy-done.4
  11.1 2.3 %shard_map.55.picked_ref = f32[8,128,256]{2,1,0:T(8,128)S(1)} custom-call(s32[4,6]{1,0:T(4,128)S(1)} %copy-done.4, bf16[128,1280]{1,0:T(8,128)(2,1)S(1)} %copy-done, bf16[128,1280]{1,0:T(8,128)(2,1)S(1)} %copy-done.1, bf16[128,1280]{1,0:T(8,128)(2,1)S(1)} %copy-done.2, bf16[128,1280]{1,0:T(8,128)(2,1)S(1)} %copy-done.3), custom_call_target="tpu_custom_call" | custom-call | tf_op jit(solution)/shard_map/pallas_call | solution.py:133
  13.4 21.4 %shard_map.56 = f32[8,128,256]{2,1,0:T(8,128)S(1)} custom-call(f32[8,128,256]{2,1,0:T(8,128)S(1)} %shard_map.55.picked_ref), custom_call_target="tpu_custom_call" | custom-call | tf_op jit(solution)/shard_map/pallas_call | solution.py:201
  34.9 48.0 %shard_map.57 = f32[256,256]{1,0:T(8,128)} custom-call(f32[1024,256]{1,0:T(8,128)S(1)} %bitcast.3), custom_call_target="tpu_custom_call" | custom-call | tf_op jit(solution)/shard_map/pallas_call | solution.py:289
  82.8 0.0 all-gather.3.cloned.1.call-update
  82.9 84.2 %all-gather.3.cloned.1.call-done = f32[8192,256]{1,0:T(8,128)} async-done(((f32[256,256]{1,0:T(8,128)}), f32[8192,256]{1,0:T(8,128)}) %all-gather.3.cloned.1.call-update) | async-done | bytes 8388624 | tf_op jit(solution)/shard_map/all_gather | solution.py:317
  167.0 0.0 copy-start.5
  167.0 0.7 copy-done.5
  167.7 5.0 %shard_map.58 = f32[24,256,256]{2,1,0:T(8,128)} custom-call(s32[4,6]{1,0:T(4,128)S(1)} %copy-done.5, f32[32,256,256]{2,1,0:T(8,128)} %bitcast.4), custom_call_target="tpu_custom_call" | custom-call | tf_op jit(solution)/shard_map/pallas_call | solution.py:268
Async XLA Ops:
  6.5 160.5 %all-gather.3.cloned.1.call-start = ((), (), s32[]{:S(2)}) async-start(), calls=%async_computation | async-start | bytes 8650752 | tf_op jit(solution)/shard_map/all_gather | solution.py:317
  6.5 1.0 copy-start
  7.5 1.0 copy-start.1
  8.5 1.0 copy-start.2
  9.5 1.0 copy-start.3
  10.4 0.7 copy-start.4
  167.0 0.7 copy-start.5
Sparse Core Ops, SparseCore 0:
  83.0 84.0 all-gather.2
